TPU v7x, 32 devices: a whole 2x2x4 slice. The times are simulated.
32 devices in a mesh: section: 4 (over y, x), mp: 2 (over core), dp: 4 (over z).
Axes of the slice: x: 2, y: 2, z: 4, core: 2. Of those that a mesh axis runs over, the one named last changes fastest.
Arguments:
- tokens: bfloat16 [512, 4096], P(('dp', 'section', 'mp')), parts along dimension 0, may hold values from -6 to 6
- mix_gain: bfloat16 [4096], replicated, may hold values from 0.099609375 to 1.8984375
- inner_weight: bfloat16 [4096, 2048], P(None, ('section', 'mp')), may hold values from -0.09375 to 0.09375
- gate_weight: bfloat16 [4096, 2048], P(None, ('section', 'mp')), may hold values from -0.09375 to 0.09375
- group_weight: bfloat16 [4096, 1024], P(None, ('section', 'mp')), may hold values from -0.09375 to 0.09375
- step_weight: bfloat16 [4096, 32], P(None, ('section', 'mp')), may hold values from -0.09375 to 0.09375
- step_bias: float32 [32], P(('section', 'mp')), may hold values from -4 to -1
- rate_log: float32 [32], P(('section', 'mp')), may hold values from -3 to 1
- skip_scale: float32 [32], P(('section', 'mp')), may hold values from 0.5 to 1.5
- norm_gain: bfloat16 [2048], P(('section', 'mp')), may hold values from 0.099609375 to 1.8984375
- out_weight: bfloat16 [2048, 4096], P(('section', 'mp')), may hold values from -0.125 to 0.125
- earlier_states: float32 [16, 2, 4, 4, 64, 256], P(('dp', 'section'), 'mp'), parts along dimension 0, may hold values from -0.8 to 0.8
- earlier_decay: float32 [16, 2, 4, 4], P(('dp', 'section'), 'mp'), parts along dimension 0, may hold values from -2 to -0.01
- attention_gain: bfloat16 [4096], replicated, may hold values from 0.099609375 to 1.8984375
- query_weight: bfloat16 [4096, 1024], P(None, ('section', 'mp')), may hold values from -1 to 1
- keyval_weight: bfloat16 [4096, 512], P(None, ('section', 'mp')), may hold values from -1 to 1
- context_weight: bfloat16 [1024, 4096], P(('section', 'mp')), may hold values from -0.1875 to 0.1875
- key_cache: bfloat16 [32768, 2, 256], P(('dp', 'section'), 'mp'), parts along dimension 0, may hold values from -6 to 6
- doc_offset: int32 [4], P('dp'), parts along dimension 0, may hold values from 1 to 8192
Outputs:
- hidden_out: bfloat16 [512, 4096], P(('dp', 'section', 'mp')), parts along dimension 0
- final_state: float32 [128, 64, 256], P(('dp', 'section', 'mp')), parts along dimension 0
- window_kv: bfloat16 [512, 2, 256], P('dp', 'mp'), parts along dimension 0
There are 4 independent parts, one for each index of `dp`. A program takes and returns all parts, laid end to end along the dimension named above; an argument that names none is the same for every part. Nothing has to cross between parts.
Inputs may be any that keep to these rules, and one draw needn't show every extreme that they name: Cache positions below 8192 minus doc_offset belong to earlier documents.
All inputs are finite; a program needn't handle non-finite values.
Results may differ from a plain program's by a relative error of at most 0.033.
Values may be sent and summed in bfloat16 or wider, within the bound.
A program may use at most 128 MiB of HBM per device.

v0:
```python
import math

import jax
import jax.numpy as jnp
from jax import lax
from jax.sharding import PartitionSpec as P

epsilon = 1e-05
precise = lax.Precision.HIGHEST
masked_low = -1e30


def rms_rows(values, gain):
    widened = values.astype(jnp.float32)
    inverse = lax.rsqrt(jnp.mean(widened * widened, axis=-1, keepdims=True) + epsilon)
    return (widened * inverse * gain.astype(jnp.float32)).astype(jnp.bfloat16)


def later_sums(values):
    return jnp.cumsum(values[::-1], axis=0)[::-1] - values


def absorb_block(highest, totals, collected, logits, live, values):
    masked = jnp.where(live, logits, masked_low)
    raised = jnp.maximum(highest, jnp.max(masked, axis=1))
    shrink = jnp.exp(highest - raised)
    weights = jnp.where(live, jnp.exp(logits - raised[:, None]), 0.0)
    totals = totals * shrink + jnp.sum(weights, axis=1)
    collected = collected * shrink[:, None] + jnp.dot(
        weights.astype(jnp.bfloat16), values, preferred_element_type=jnp.float32
    )
    return (raised, totals, collected)


def local(
    tokens,
    mix_gain,
    inner_weight,
    gate_weight,
    group_weight,
    step_weight,
    step_bias,
    rate_log,
    skip_scale,
    norm_gain,
    out_weight,
    earlier_states,
    earlier_decay,
    attention_gain,
    query_weight,
    keyval_weight,
    context_weight,
    key_cache,
    doc_offset,
):
    sections = lax.axis_size("section")
    inner_width = inner_weight.shape[1]
    heads_here = step_weight.shape[1]
    head_size = inner_width // heads_here
    group_piece = group_weight.shape[1]
    first_weight = jnp.concatenate([inner_weight, gate_weight, group_weight, step_weight], axis=1)
    second_weight = jnp.concatenate([query_weight, keyval_weight], axis=1)
    normed = rms_rows(tokens, mix_gain)
    first = jnp.dot(
        lax.all_gather(normed, ("section", "mp"), axis=0, tiled=True),
        first_weight,
        preferred_element_type=jnp.float32,
    )
    window = first.shape[0]
    inner = first[:, :inner_width].astype(jnp.bfloat16)
    gates = first[:, inner_width : 2 * inner_width]
    group_part = first[:, 2 * inner_width : 2 * inner_width + group_piece].astype(jnp.bfloat16)
    step_sizes = jax.nn.softplus(first[:, 2 * inner_width + group_piece :] + step_bias)
    paired = lax.all_gather(group_part, "section", axis=1, tiled=True)
    state_size = paired.shape[1] // 2
    writer = paired[:, :state_size]
    reader = paired[:, state_size:]
    local_states = earlier_states[:, 0]
    local_decay = earlier_decay[:, 0]
    moved_states, moved_decay = (
        lax.all_to_all(
            local_states.astype(jnp.bfloat16), "section", split_axis=1, concat_axis=0, tiled=True
        ).astype(local_states.dtype),
        lax.all_to_all(
            local_decay.astype(jnp.bfloat16), "section", split_axis=1, concat_axis=0, tiled=True
        ).astype(local_decay.dtype),
    )
    after_own = later_sums(moved_decay[:, 0])
    start_state = jnp.einsum(
        "ch,chpn->hpn", jnp.exp(after_own), moved_states[:, 0], precision=precise
    )
    rates = -jnp.exp(rate_log)
    log_decay = jnp.cumsum(step_sizes * rates, axis=0)
    position = jnp.arange(window, dtype=jnp.int32)
    causal = position[:, None] >= position[None, :]
    affinity = jnp.dot(reader, writer.T, preferred_element_type=jnp.float32)
    decay_cols = log_decay.T
    spread = decay_cols[:, :, None] - decay_cols[:, None, :]
    mixing = jnp.where(
        causal[None],
        affinity[None] * jnp.exp(jnp.where(causal[None], spread, 0.0)) * step_sizes.T[:, None, :],
        0.0,
    ).astype(jnp.bfloat16)
    inputs_heads = inner.reshape(window, heads_here, head_size)
    intra = jnp.einsum("htu,uhp->thp", mixing, inputs_heads, preferred_element_type=jnp.float32)
    widened = inputs_heads.astype(jnp.float32)
    carried = (
        jnp.einsum("tn,hpn->thp", reader.astype(jnp.float32), start_state, precision=precise)
        * jnp.exp(log_decay)[:, :, None]
    )
    mamba_y = intra + carried + skip_scale[None, :, None] * widened
    last_decay = log_decay[-1]
    tail_weights = jnp.exp(last_decay[None, :] - log_decay) * step_sizes
    final_state = jnp.exp(last_decay)[:, None, None] * start_state + jnp.einsum(
        "th,thp,tn->hpn", tail_weights, widened, writer.astype(jnp.float32), precision=precise
    )
    gated = mamba_y * jax.nn.silu(gates.reshape(window, heads_here, head_size))
    row_squares = jnp.sum(jnp.sum(gated * gated, axis=2), axis=1)
    group_squares = lax.psum(row_squares, "section")
    inverse = lax.rsqrt(group_squares / (sections * inner_width) + epsilon)
    normed_heads = (
        (
            gated
            * inverse[:, None, None]
            * norm_gain.astype(jnp.float32).reshape(heads_here, head_size)
        )
        .astype(jnp.bfloat16)
        .reshape(window, inner_width)
    )
    mamba_out = lax.psum_scatter(
        jnp.dot(normed_heads, out_weight, preferred_element_type=jnp.float32).astype(jnp.bfloat16),
        ("section", "mp"),
        scatter_dimension=0,
        tiled=True,
    ).astype(jnp.float32)
    residual = (tokens.astype(jnp.float32) + mamba_out).astype(jnp.bfloat16)
    normed_two = rms_rows(residual, attention_gain)
    second = jnp.dot(
        lax.all_gather(normed_two, ("section", "mp"), axis=0, tiled=True),
        second_weight,
        preferred_element_type=jnp.float32,
    )
    head_width = query_weight.shape[1]
    query = second[:, :head_width].astype(jnp.bfloat16)
    keyval_part = second[:, head_width:].astype(jnp.bfloat16)
    keyval_group = lax.all_gather(keyval_part, "section", axis=1, tiled=True)
    keys_new = keyval_group[:, :head_width]
    values_new = keyval_group[:, head_width:]
    scale = 1.0 / math.sqrt(head_width)
    cache_here = key_cache[:, 0]
    cache_rows = cache_here.shape[0]
    first_valid = cache_rows * sections - doc_offset[0]
    piece = lax.all_gather(cache_here, "section", axis=0, tiled=True)
    highest = jnp.full((window,), masked_low, jnp.float32)
    totals = jnp.zeros((window,), jnp.float32)
    collected = jnp.zeros((window, head_width), jnp.float32)
    logits = jnp.dot(query, piece[:, :head_width].T, preferred_element_type=jnp.float32) * scale
    live = jnp.arange(piece.shape[0], dtype=jnp.int32) >= first_valid
    highest, totals, collected = absorb_block(
        highest, totals, collected, logits, live[None, :], piece[:, head_width:]
    )
    logits_new = jnp.dot(query, keys_new.T, preferred_element_type=jnp.float32) * scale
    highest, totals, collected = absorb_block(
        highest, totals, collected, logits_new, causal, values_new
    )
    context = (collected / totals[:, None]).astype(jnp.bfloat16)
    attention_out = lax.psum_scatter(
        jnp.dot(context, context_weight, preferred_element_type=jnp.float32).astype(jnp.bfloat16),
        ("section", "mp"),
        scatter_dimension=0,
        tiled=True,
    ).astype(jnp.float32)
    hidden_out = (residual.astype(jnp.float32) + attention_out).astype(jnp.bfloat16)
    return (hidden_out, final_state, keyval_group[:, None, :])


def solution(mesh):
    in_specs = (
        P(("dp", "section", "mp"), None),
        P(),
        P(None, ("section", "mp")),
        P(None, ("section", "mp")),
        P(None, ("section", "mp")),
        P(None, ("section", "mp")),
        P(("section", "mp")),
        P(("section", "mp")),
        P(("section", "mp")),
        P(("section", "mp")),
        P(("section", "mp"), None),
        P(("dp", "section"), "mp", None, None, None, None),
        P(("dp", "section"), "mp", None, None),
        P(),
        P(None, ("section", "mp")),
        P(None, ("section", "mp")),
        P(("section", "mp"), None),
        P(("dp", "section"), "mp", None),
        P("dp"),
    )
    out_specs = (
        P(("dp", "section", "mp"), None),
        P(("dp", "section", "mp"), None, None),
        P("dp", "mp", None),
    )
    return jax.shard_map(local, mesh=mesh, in_specs=in_specs, out_specs=out_specs, check_vma=False)
```

profile of v0, /device:TPU:0, one launch (start us, length us, event | category | flops | bytes accessed | tf_op | source)
XLA Modules:
  0.0 232.7 jit_solution(3981221735241817918)
XLA Ops:
  7.2 1.2 fusion.41
  9.1 1.7 fusion.43
  12.1 5.2 %all-to-all-start = ((bf16[1,4,4]{2,0,1:T(2,128)(2,1)}), bf16[1,4,4]{2,0,1:T(2,128)(2,1)S(1)}, u32[]{:S(2)}, u32[]{:S(2)}) async-start(bf16[1,4,4]{2,0,1:T(2,128)(2,1)} %copy.38), calls=%async_computation | async-start | bytes 4096 | tf_op jit(solution)/shard_map/all_to_all | solution.py:84
  18.1 2.2 copy.33
  20.3 2.1 convert_bitcast_fusion
  22.4 4.2 %all-to-all-start.1 = ((bf16[1,4,4,64,256]{4,3,2,0,1:T(8,128)(2,1)}), bf16[1,4,4,64,256]{4,3,2,0,1:T(8,128)(2,1)S(1)}, u32[]{:S(2)}, u32[]{:S(2)}) async-start(bf16[1,4,4,64,256]{4,3,2,0,1:T(8,128)(2,1)} %convert_bitcast_fusion), calls=%async_computation.1 | async-start | bytes 1048576 | tf_op jit(solution)/shard_map/all_to_all | solution.py:81
  26.9 9.7 %all-to-all-done.1 = bf16[1,4,4,64,256]{4,3,2,0,1:T(8,128)(2,1)S(1)} async-done(((bf16[1,4,4,64,256]{4,3,2,0,1:T(8,128)(2,1)}), bf16[1,4,4,64,256]{4,3,2,0,1:T(8,128)(2,1)S(1)}, u32[]{:S(2)}, u32[]{:S(2)}) %all-to-all-start.1) | async-done | bytes 524320 | tf_op jit(solution)/shard_map/all_to_all | solution.py:81
  36.5 1.0 fusion.39
  38.4 5.6 %fusion.88 = (bf16[128,644]{0,1:T(8,128)(2,1)S(1)}, f32[128,644]{0,1:T(8,128)S(1)}) fusion(bf16[128,4096]{1,0:T(8,128)(2,1)} %all-gather.5.cloned.1.call-done, bf16[4096,4]{1,0:T(8,128)(2,1)} %copy.33, bf16[4096,128]{1,0:T(8,128)(2,1)} %param.23, bf16[4096,256]{1,0:T(8,128)(2,1)} %param.22, bf16[4096,256]{1,0:T(8,128)(2,1)} %param.21), kind=kOutput, calls=%fused_computation.113 | convolution fusion | flops 696467968 | bytes 6818816 | tf_op jit(solution)/shard_map/dot_general | solution.py:64
  44.7 8.4 %all_gather.16 = bf16[128,512]{0,1:T(8,128)(2,1)S(1)} all-gather(bf16[128,128]{0,1:T(8,128)(2,1)S(1)} %slice.57), channel_id=1, replica_groups=mesh['section'=4,'mp'=2,'dp'=4] {'section'}, dimensions={1}, use_global_device_ids=true | all-gather | bytes 163840 | tf_op jit(solution)/shard_map/all_gather | solution.py:74
  54.0 8.9 %psum.7 = f32[128]{0:T(128)S(1)} all-reduce(f32[128]{0:T(128)S(1)} %get-tuple-element.18), channel_id=1, replica_groups=mesh['section'=4,'mp'=2,'dp'=4] {'section'}, use_global_device_ids=true, to_apply=%region_4.5 | all-reduce | flops 128 | bytes 1024 | tf_op jit(solution)/shard_map/psum | solution.py:119
  63.1 1.4 convolution_convert_fusion.1
  64.6 35.5 %reduce-scatter.3.cloned.1.call-done = bf16[16,4096]{1,0:T(8,128)(2,1)} async-done(((bf16[128,4096]{1,0:T(8,128)(2,1)}), bf16[16,4096]{1,0:T(8,128)(2,1)}) %reduce-scatter.3.cloned.1.call-update) | async-done | bytes 131088 | tf_op jit(solution)/shard_map/reduce_scatter | solution.py:130
  100.1 1.1 fusion.45
  101.2 1.7 fusion.47
  104.1 1.5 copy.41
  105.7 20.8 %all-gather.7.cloned.1.call-done = bf16[128,4096]{1,0:T(8,128)(2,1)} async-done(((bf16[16,4096]{1,0:T(8,128)(2,1)}), bf16[128,4096]{1,0:T(8,128)(2,1)}) %all-gather.7.cloned.1.call-update) | async-done | bytes 1048592 | tf_op jit(solution)/shard_map/all_gather | solution.py:139
  126.5 2.4 %fusion.24 = bf16[128,192]{0,1:T(8,128)(2,1)S(1)} fusion(bf16[128,4096]{1,0:T(8,128)(2,1)} %all-gather.7.cloned.1.call-done, bf16[4096,64]{1,0:T(8,128)(2,1)S(1)} %copy.41, bf16[4096,128]{1,0:T(8,128)(2,1)} %param.33), kind=kOutput, calls=%fused_computation.31 | convolution fusion | flops 204496896 | bytes 2670592 | tf_op jit(solution)/shard_map/dot_general | solution.py:138
  128.9 8.2 %all_gather.19 = bf16[128,256]{0,1:T(8,128)(2,1)S(1)} all-gather(bf16[128,64]{0,1:T(8,128)(2,1)S(1)} %slice.65), channel_id=1, replica_groups=mesh['section'=4,'mp'=2,'dp'=4] {'section'}, dimensions={1}, use_global_device_ids=true | all-gather | bytes 81920 | tf_op jit(solution)/shard_map/all_gather | solution.py:146
  137.3 43.6 %all-gather.9.cloned.1.call-done = bf16[8192,1,256]{2,0,1:T(8,128)(2,1)} async-done(((bf16[2048,1,256]{2,0,1:T(8,128)(2,1)}), bf16[8192,1,256]{2,0,1:T(8,128)(2,1)}) %all-gather.9.cloned.1.call-update) | async-done | bytes 4194320 | tf_op jit(solution)/shard_map/all_gather | solution.py:153
  180.9 2.6 %select_reduce_fusion = (f32[128]{0:T(128)S(1)}, f32[128,8192]{1,0:T(8,128)S(1)}) fusion(pred[8192]{0:T(1024)(128)(4,1)S(1)} %iota_compare_fusion.1, bf16[8192,256]{1,0:T(8,128)(2,1)} %bitcast.48, bf16[128,192]{0,1:T(8,128)(2,1)} %copy-done.6), kind=kOutput, calls=%fused_computation.12 | convolution fusion | flops 271581056 | bytes 6332928 | tf_op jit(solution)/shard_map/dot_general | solution.py:157
  185.5 2.8 %convolution_convert_fusion = bf16[128,4096]{1,0:T(8,128)(2,1)} fusion(bf16[128,4096]{1,0:T(8,128)(2,1)} %param.35, f32[128,128]{1,0:T(8,128)S(1)} %fusion.33, f32[128,128]{0,1:T(8,128)S(1)} %get-tuple-element.23, bf16[128,256]{0,1:T(8,128)(2,1)S(1)} %all_gather.19, f32[128]{0:T(128)S(1)} %get-tuple-element.9, f32[128]{0:T(128)S(1)} %get-tuple-element.14), kind=kOutput, calls=%fused_computation.9 | convolution fusion | flops 139051008 | bytes 2262016 | tf_op jit(solution)/shard_map/dot_general | solution.py:168
  190.1 34.5 %reduce-scatter.5.cloned.1.call-done = bf16[16,4096]{1,0:T(8,128)(2,1)} async-done(((bf16[128,4096]{1,0:T(8,128)(2,1)}), bf16[16,4096]{1,0:T(8,128)(2,1)}) %reduce-scatter.5.cloned.1.call-update) | async-done | bytes 131088 | tf_op jit(solution)/shard_map/reduce_scatter | solution.py:167
  224.6 1.6 fusion.48
  (78 shorter events, 10.3 us)
Async XLA Ops:
  7.2 55.9 %copy-start = (bf16[256,4096]{1,0:T(8,128)(2,1)S(1)}, bf16[256,4096]{1,0:T(8,128)(2,1)}, u32[]{:S(2)}) copy-start(bf16[256,4096]{1,0:T(8,128)(2,1)} %param.29) | copy-start | bytes 6291460
  7.2 19.5 %copy-start.9 = (f32[4]{0:T(128)S(1)}, f32[4]{0:T(128)}, u32[]{:S(2)}) copy-start(f32[4]{0:T(128)} %param.26) | copy-start | bytes 52
  7.2 31.2 %all-gather.5.cloned.1.call-start = ((), (), s32[]{:S(2)}) async-start(), calls=%async_computation.4 | async-start | bytes 1179648 | tf_op jit(solution)/shard_map/all_gather | solution.py:65
  12.1 10.4 %all-to-all-start = ((bf16[1,4,4]{2,0,1:T(2,128)(2,1)}), bf16[1,4,4]{2,0,1:T(2,128)(2,1)S(1)}, u32[]{:S(2)}, u32[]{:S(2)}) async-start(bf16[1,4,4]{2,0,1:T(2,128)(2,1)} %copy.38), calls=%async_computation | async-start | bytes 4096 | tf_op jit(solution)/shard_map/all_to_all | solution.py:84
  22.4 14.1 %all-to-all-start.1 = ((bf16[1,4,4,64,256]{4,3,2,0,1:T(8,128)(2,1)}), bf16[1,4,4,64,256]{4,3,2,0,1:T(8,128)(2,1)S(1)}, u32[]{:S(2)}, u32[]{:S(2)}) async-start(bf16[1,4,4,64,256]{4,3,2,0,1:T(8,128)(2,1)} %convert_bitcast_fusion), calls=%async_computation.1 | async-start | bytes 1048576 | tf_op jit(solution)/shard_map/all_to_all | solution.py:81
  26.6 73.5 %reduce-scatter.3.cloned.1.call-start = ((), (), s32[]{:S(2)}) async-start(), calls=%async_computation.5 | async-start | bytes 1179648 | tf_op jit(solution)/shard_map/reduce_scatter | solution.py:130
  37.5 15.9 %copy-start.3 = (f32[4,1,64,256]{3,1,2,0:T(1,128)}, f32[4,1,64,256]{3,1,2,0:T(1,128)S(1)}, u32[]{:S(2)}) copy-start(f32[4,1,64,256]{3,1,2,0:T(1,128)S(1)} %fusion.39) | copy-start | bytes 786436
  37.6 6.5 %copy-start.8 = (f32[4]{0:T(128)S(1)}, f32[4]{0:T(128)}, u32[]{:S(2)}) copy-start(f32[4]{0:T(128)} %param.25) | copy-start | bytes 52
  37.6 16.1 %copy-start.10 = (f32[4]{0:T(128)S(1)}, f32[4]{0:T(128)}, u32[]{:S(2)}) copy-start(f32[4]{0:T(128)} %param.27) | copy-start | bytes 52
  44.0 20.6 %copy-start.7 = (bf16[4096]{0:T(1024)(128)(2,1)S(1)}, bf16[4096]{0:T(1024)(128)(2,1)}, u32[]{:S(2)}) copy-start(bf16[4096]{0:T(1024)(128)(2,1)} %param.32) | copy-start | bytes 24580
  44.0 56.1 %copy-start.1 = (bf16[16,4096]{1,0:T(8,128)(2,1)S(1)}, bf16[16,4096]{1,0:T(8,128)(2,1)}, u32[]{:S(2)}) copy-start(bf16[16,4096]{1,0:T(8,128)(2,1)} %param.19) | copy-start | bytes 393220
  64.5 61.9 %all-gather.7.cloned.1.call-start = ((), (), s32[]{:S(2)}) async-start(), calls=%async_computation.6 | async-start | bytes 1179648 | tf_op jit(solution)/shard_map/all_gather | solution.py:139
  102.9 78.1 %all-gather.9.cloned.1.call-start = ((), (), s32[]{:S(2)}) async-start(), calls=%async_computation.8 | async-start | bytes 5242880 | tf_op jit(solution)/shard_map/all_gather | solution.py:153
  103.4 121.1 %reduce-scatter.5.cloned.1.call-start = ((), (), s32[]{:S(2)}) async-start(), calls=%async_computation.7 | async-start | bytes 1179648 | tf_op jit(solution)/shard_map/reduce_scatter | solution.py:167
  128.9 8.2 %copy-start.6 = (bf16[128,192]{0,1:T(8,128)(2,1)}, bf16[128,192]{0,1:T(8,128)(2,1)S(1)}, u32[]{:S(2)}) copy-start(bf16[128,192]{0,1:T(8,128)(2,1)S(1)} %fusion.24) | copy-start | bytes 147460
  180.9 3.7 %copy-start.5 = (bf16[8192,1,256]{2,0,1:T(8,128)(2,1)S(1)}, bf16[8192,1,256]{2,0,1:T(8,128)(2,1)}, u32[]{:S(2)}) copy-start(bf16[8192,1,256]{2,0,1:T(8,128)(2,1)} %all-gather.9.cloned.1.call-done) | copy-start | bytes 12582916
  184.6 3.8 %copy-start.4 = (f32[4,1,64,256]{3,1,2,0:T(1,128)S(1)}, f32[4,1,64,256]{3,1,2,0:T(1,128)}, u32[]{:S(2)}) copy-start(f32[4,1,64,256]{3,1,2,0:T(1,128)} %copy-done.3) | copy-start | bytes 786436
  184.6 40.0 %copy-start.2 = (bf16[16,4096]{1,0:T(8,128)(2,1)S(1)}, bf16[16,4096]{1,0:T(8,128)(2,1)}, u32[]{:S(2)}) copy-start(bf16[16,4096]{1,0:T(8,128)(2,1)} %reduce-scatter.3.cloned.1.call-done) | copy-start | bytes 393220
Sparse Core Ops, SparseCore 0:
  10.9 27.4 all-gather.4
  64.7 35.3 reduce-scatter.2
  103.0 23.4 all-gather.6
  128.2 52.6 all-gather.8
  188.5 36.0 reduce-scatter.4
where the time goes:
time: 233 us
  waiting for transfers between devices  145 us (62%)
  blocking collectives  25.5 us (11%)
  matrix products  18.7 us (8%)
  between operations  14.7 us (6%)
  other arithmetic  12.3 us (5%)
  starting transfers between devices  9.51 us (4%)
  local copies, waits for them, and re-layouts  6.51 us (3%)
    all_gather x1, waiting for transfers between devices, local(): piece = lax.all_gather(cache_here, 'section', axis=0, tiled=True)  43.6 us
    reduce_scatter x1, waiting for transfers between devices, local(): lax.psum_scatter(jnp.dot(normed_heads, out_weight, preferred_element_type...  35.5 us
    reduce_scatter x1, waiting for transfers between devices, local(): lax.psum_scatter(jnp.dot(context, context_weight, preferred_element_type=...  34.5 us
    all_gather x1, waiting for transfers between devices, local(): lax.all_gather(normed_two, ('section', 'mp'), axis=0, tiled=True)  20.8 us
    all_to_all x1, waiting for transfers between devices, local(): lax.all_to_all(local_states.astype(jnp.bfloat16), 'section', split_axis=1...  9.65 us
    psum x1, blocking collectives, local(): group_squares = lax.psum(row_squares, 'section')  8.92 us
    all_gather x1, blocking collectives, local(): paired = lax.all_gather(group_part, 'section', axis=1, tiled=True)  8.41 us
    all_gather x1, blocking collectives, local(): keyval_group = lax.all_gather(keyval_part, 'section', axis=1, tiled=True)  8.19 us
  transfers between devices with their start and end apart: 7, of which 6 were waited for; matrix products, arithmetic and copies ran while one was open for 6% of the time, Pallas kernels for 0%

commit v1 on v0

v1 whole, which is shorter than its diff:
```python
import functools
import math

import jax
import jax.numpy as jnp
from jax import lax
from jax.experimental import pallas as pl
from jax.experimental.pallas import tpu as pltpu
from jax.sharding import PartitionSpec as P

epsilon = 1e-05
masked_low = -1e30
MESH = pl.DeviceIdType.MESH
f32 = jnp.float32
bf16 = jnp.bfloat16
CHUNKS = 4


def dot(a, b, ca, cb, **kw):
    return lax.dot_general(a, b, (((ca,), (cb,)), ((), ())), preferred_element_type=f32, **kw)


def kernel(
    S, MP,
    tokens, mix_gain, inner_w, gate_w, group_w, step_w, step_bias, rate_log, skip_scale, norm_gain,
    out_w, states, decay, att_gain, query_w, keyval_w, context_w, cache, doc_offset,
    hidden, final_state, window_kv,
    W1, WS, Wo, W2, WKV, Wc, CK, SF, load_sem,
    G1, G2, g1s, g1r, g2s, g2r,
    acc, GP, gps, gpr, STS, ST, sts, str_, DB, dbs, dbr, SQ, sqs, sqr,
    SND1, RCV1, r1s, r1r, MID1, RCM1, m1s, m1r,
    SND2, RCV2, r2s, r2r, MID2, RCM2, m2s, m2r,
    RES, QB, qbs, qbr, KVB, kvs, kvr, ACS, ACR, acs, acr, LS, LR, lss, lsr,
):
    me = lax.axis_index("section")
    mm = lax.axis_index("mp")
    rows, D = tokens.shape
    T = rows * S * MP
    KC = D // CHUNKS
    IW = inner_w.shape[1]
    GW = group_w.shape[1]
    heads = step_w.shape[1]
    HP = IW // heads
    HD = query_w.shape[1]
    KW = keyval_w.shape[1]
    sent = []

    def sec(i):
        return lax.rem(me + i + S, S)

    def core(j):
        return lax.rem(mm + j + MP, MP)

    def rcopy(src, dst, ss, rs, **where):
        return pltpu.make_async_remote_copy(
            src_ref=src, dst_ref=dst, send_sem=ss, recv_sem=rs, device_id=where, device_id_type=MESH
        )

    def send(src, dst, ss, rs, **where):
        d = rcopy(src, dst, ss, rs, **where)
        d.start()
        sent.append(d)

    def arrive(dst, ss, rs, **where):
        rcopy(dst, dst, ss, rs, **where).wait_recv()

    loads = [
        (inner_w, W1.at[:, 0:IW]),
        (gate_w, W1.at[:, IW : 2 * IW]),
        (group_w, W1.at[:, 2 * IW : 2 * IW + GW]),
        (step_w, WS),
        (states.at[0, 0], SF),
        (out_w, Wo),
        (query_w, W2.at[:, 0:HD]),
        (keyval_w, WKV),
        (cache, CK),
        (context_w, Wc),
    ]
    copies = [pltpu.make_async_copy(a, b, load_sem.at[k]) for k, (a, b) in enumerate(loads)]
    for c in copies:
        c.start()

    barrier = pltpu.get_barrier_semaphore()
    for i in range(1, S):
        pl.semaphore_signal(barrier, inc=1, device_id={"section": sec(i)}, device_id_type=MESH)
    for j in range(1, MP):
        pl.semaphore_signal(barrier, inc=1, device_id={"mp": core(j)}, device_id_type=MESH)

    def norm_into(G, values, gain):
        inverse = lax.rsqrt(jnp.mean(values * values, axis=-1, keepdims=True) + epsilon)
        n = (values * inverse * gain).astype(bf16)
        for c in range(CHUNKS):
            G[c, me, mm] = n[:, c * KC : (c + 1) * KC]

    def gather_start(G, ss, rs):
        for c in range(CHUNKS):
            own = G.at[c, me, mm]
            for i in range(1, S):
                send(own, own, ss.at[c, i - 1], rs.at[c, i - 1], section=sec(i))
            for j in range(1, MP):
                k = S - 1 + (j - 1) * S
                send(own, own, ss.at[c, k], rs.at[c, k], mp=core(j))

    def gather_chunk(G, ss, rs, c):
        for i in range(1, S):
            got = G.at[c, sec(-i), mm]
            arrive(got, ss.at[c, i - 1], rs.at[c, i - 1], section=sec(i))
            for j in range(1, MP):
                k = S - 1 + (j - 1) * S + i
                send(got, got, ss.at[c, k], rs.at[c, k], mp=core(j))
        for j in range(1, MP):
            for i in range(S):
                k = S - 1 + (j - 1) * S + i
                got = G.at[c, sec(-i), core(-j)]
                arrive(got, ss.at[c, k], rs.at[c, k], mp=core(j))

    norm_into(G1, tokens[...].astype(f32), mix_gain[...].astype(f32))
    DB[me] = jnp.zeros(DB.shape[1:], f32)
    DB[me, 0:S, 0:heads] = decay[0, 0]
    pl.semaphore_wait(barrier, S - 1 + MP - 1)
    gather_start(G1, g1s, g1r)

    copies[4].wait()
    for q in range(S):
        STS[q] = SF[q].reshape(IW, SF.shape[-1]).astype(bf16)
    ST[me] = STS[me]
    for i in range(1, S):
        send(DB.at[me], DB.at[me], dbs.at[i - 1], dbr.at[i - 1], section=sec(i))
        send(STS.at[sec(i)], ST.at[me], sts.at[i - 1], str_.at[i - 1], section=sec(i))

    copies[3].wait()
    W1[:, 2 * IW + GW :] = jnp.zeros((D, W1.shape[1] - 2 * IW - GW), bf16)
    W1[:, 2 * IW + GW : 2 * IW + GW + heads] = WS[...]
    copies[7].wait()
    W2[:, HD:] = jnp.zeros((D, W2.shape[1] - HD), bf16)
    W2[:, HD : HD + KW] = WKV[...]
    for k in (0, 1, 2):
        copies[k].wait()

    def project(G, ss, rs, W):
        total = None
        for c in range(CHUNKS):
            gather_chunk(G, ss, rs, c)
            part = jnp.dot(
                G[c].reshape(T, KC), W[c * KC : (c + 1) * KC, :], preferred_element_type=f32
            )
            if c == 0:
                acc[:, 0 : W.shape[1]] = part
            else:
                acc[:, 0 : W.shape[1]] += part

    project(G1, g1s, g1r, W1)
    GP[me] = acc[:, 2 * IW : 2 * IW + GW].astype(bf16)
    for i in range(1, S):
        send(GP.at[me], GP.at[me], gps.at[i - 1], gpr.at[i - 1], section=sec(i))

    lane = lax.broadcasted_iota(jnp.int32, (1, 128), 1)
    wide = lax.broadcasted_iota(jnp.int32, (1, IW), 1) // HP

    def spread_scalars(ref, index):
        row = jnp.zeros(index.shape, f32)
        for h in range(heads):
            row = jnp.where(index == h, ref[h], row)
        return row

    def expand(cols):
        full = jnp.broadcast_to(cols[:, 0:1], (cols.shape[0], IW))
        for h in range(1, heads):
            full = jnp.where(wide == h, cols[:, h : h + 1], full)
        return full

    x = acc[:, 2 * IW + GW : 2 * IW + GW + 128] + spread_scalars(step_bias, lane)
    step = jnp.maximum(x, 0.0) + jnp.log1p(jnp.exp(-jnp.abs(x)))
    rates = -jnp.exp(spread_scalars(rate_log, lane))
    t_row = lax.broadcasted_iota(jnp.int32, (T, T), 0)
    t_col = lax.broadcasted_iota(jnp.int32, (T, T), 1)
    causal = t_row >= t_col
    log_decay = jnp.dot(
        causal.astype(f32), step * rates, preferred_element_type=f32, precision=lax.Precision.HIGHEST
    )
    ld_rows = log_decay.T
    st_rows = step.T
    inner = acc[:, 0:IW].astype(bf16)
    inner_f = inner.astype(f32)
    gates = acc[:, IW : 2 * IW]
    silu = gates / (1.0 + jnp.exp(-gates))
    skip = spread_scalars(skip_scale, wide) * inner_f
    reach = expand(jnp.exp(log_decay))

    for i in range(1, S):
        arrive(DB.at[sec(-i)], dbs.at[i - 1], dbr.at[i - 1], section=sec(i))
        arrive(ST.at[sec(-i)], sts.at[i - 1], str_.at[i - 1], section=sec(i))
    later = jnp.zeros((1, 128), f32)
    factors = [None] * S
    for c in reversed(range(S)):
        factors[c] = jnp.exp(later)
        later = later + DB[c, pl.ds(me, 1), :]
    for h in range(heads):
        total = factors[0][:, h : h + 1] * ST[0, h * HP : (h + 1) * HP, :].astype(f32)
        for c in range(1, S):
            total += factors[c][:, h : h + 1] * ST[c, h * HP : (h + 1) * HP, :].astype(f32)
        final_state[h] = total
    start = jnp.concatenate([final_state[h].astype(bf16) for h in range(heads)], axis=0)

    for i in range(1, S):
        arrive(GP.at[sec(-i)], gps.at[i - 1], gpr.at[i - 1], section=sec(i))
    writer = jnp.concatenate([GP[s] for s in range(S // 2)], axis=1)
    reader = jnp.concatenate([GP[s] for s in range(S // 2, S)], axis=1)
    affinity = dot(reader, writer, 1, 1)
    y = dot(reader, start, 1, 1) * reach + skip
    intra = jnp.zeros((T, IW), f32)
    for h in range(heads):
        gap = jnp.where(causal, log_decay[:, h : h + 1] - ld_rows[h : h + 1, :], 0.0)
        mixing = jnp.where(causal, affinity * jnp.exp(gap) * st_rows[h : h + 1, :], 0.0).astype(bf16)
        intra = jnp.where(wide == h, jnp.dot(mixing, inner, preferred_element_type=f32), intra)
    gated = (y + intra) * silu
    SQ[me] = dot(jnp.ones((8, IW), f32), gated * gated, 1, 1, precision=lax.Precision.HIGHEST)
    for i in range(1, S):
        send(SQ.at[me], SQ.at[me], sqs.at[i - 1], sqr.at[i - 1], section=sec(i))
    lhs = (gated * norm_gain[...].astype(f32)).astype(bf16)

    def reduce_send(SND, ss, rs, c, value):
        value = value.astype(bf16).reshape(S, MP, rows, KC)
        for s in range(S):
            for m in range(MP):
                SND[c, m, s] = value[s, m]

    def scatter_pairs(SND, RCV, ss, rs, c):
        for j in range(1, MP):
            send(SND.at[c, core(j)], RCV.at[c, j - 1], ss.at[c, j - 1], rs.at[c, j - 1], mp=core(j))

    def scatter_sections(SND, RCV, ss, rs, MID, RCM, ms, mr, c):
        for j in range(1, MP):
            arrive(RCV.at[c, j - 1], ss.at[c, j - 1], rs.at[c, j - 1], mp=core(j))
        total = SND[c, mm].astype(f32)
        for j in range(1, MP):
            total += RCV[c, j - 1].astype(f32)
        MID[c] = total.astype(bf16)
        for i in range(1, S):
            send(MID.at[c, sec(i)], RCM.at[c, i - 1], ms.at[c, i - 1], mr.at[c, i - 1], section=sec(i))

    def scatter_end(MID, RCM, ms, mr, c):
        total = MID[c, me].astype(f32)
        for i in range(1, S):
            arrive(RCM.at[c, i - 1], ms.at[c, i - 1], mr.at[c, i - 1], section=sec(i))
            total += RCM[c, i - 1].astype(f32)
        return total

    copies[5].wait()
    inverse = None
    for c in range(CHUNKS):
        value = jnp.dot(lhs, Wo[:, c * KC : (c + 1) * KC], preferred_element_type=f32)
        if inverse is None:
            squares = SQ[me]
            for i in range(1, S):
                arrive(SQ.at[sec(-i)], sqs.at[i - 1], sqr.at[i - 1], section=sec(i))
                squares += SQ[sec(-i)]
            inverse = lax.rsqrt(squares / (S * IW) + epsilon)
            inverse = jnp.broadcast_to(inverse[0:1, :], (128, T)).T[:, 0:1]
        reduce_send(SND1, r1s, r1r, c, value * inverse)
        scatter_pairs(SND1, RCV1, r1s, r1r, c)
        if c:
            scatter_sections(SND1, RCV1, r1s, r1r, MID1, RCM1, m1s, m1r, c - 1)
    scatter_sections(SND1, RCV1, r1s, r1r, MID1, RCM1, m1s, m1r, CHUNKS - 1)

    tail = jnp.exp(log_decay[T - 1 : T, :] - log_decay) * step
    added = dot((inner_f * expand(tail)).astype(bf16), writer, 0, 0)
    last = jnp.exp(log_decay[T - 1 : T, :])
    for h in range(heads):
        final_state[h] = last[:, h : h + 1] * final_state[h] + added[h * HP : (h + 1) * HP, :]

    for c in range(CHUNKS):
        cols = slice(c * KC, (c + 1) * KC)
        RES[:, cols] = (
            tokens[:, cols].astype(f32) + scatter_end(MID1, RCM1, m1s, m1r, c)
        ).astype(bf16)
    norm_into(G2, RES[...].astype(f32), att_gain[...].astype(f32))
    gather_start(G2, g2s, g2r)
    copies[6].wait()
    copies[8].wait()
    project(G2, g2s, g2r, W2)
    QB[me] = acc[:, 0:HD].astype(bf16)
    for i in range(1, S):
        send(QB.at[me], QB.at[me], qbs.at[i - 1], qbr.at[i - 1], section=sec(i))
    KVB[me] = acc[:, HD : 2 * HD].astype(bf16)
    for i in range(1, S):
        send(KVB.at[me], KVB.at[me], kvs.at[i - 1], kvr.at[i - 1], section=sec(i))

    scale = 1.0 / math.sqrt(HD)
    held = CK.shape[0]
    position = lax.broadcasted_iota(jnp.int32, (held, 1), 0) + me * held
    bias = jnp.where(position >= held * S - doc_offset[0], 0.0, masked_low).astype(f32)

    def attend(q, keys, values, low):
        logits = dot(keys, q, 1, 1) + low
        top = jnp.max(logits, axis=0, keepdims=True)
        weights = jnp.exp((logits - top) * scale)
        total = jnp.sum(weights, axis=0, keepdims=True)
        out = dot(values, weights.astype(bf16), 0, 0)
        return top * scale, total, out

    def cached(q):
        return attend(q, CK[:, 0:HD], CK[:, HD : 2 * HD], bias)

    for i in range(1, S):
        slot = sec(-i)
        arrive(QB.at[slot], qbs.at[i - 1], qbr.at[i - 1], section=sec(i))
        top, total, out = cached(QB[slot])
        ACS[i - 1] = (out / total).astype(bf16)
        LS[i - 1, 0:8] = jnp.broadcast_to(top, (8, T))
        LS[i - 1, 8:16] = jnp.broadcast_to(total, (8, T))
        send(LS.at[i - 1], LR.at[i - 1], lss.at[i - 1], lsr.at[i - 1], section=slot)
        send(ACS.at[i - 1], ACR.at[i - 1], acs.at[i - 1], acr.at[i - 1], section=slot)
    parts = [cached(QB[me])]
    for i in range(1, S):
        arrive(KVB.at[sec(-i)], kvs.at[i - 1], kvr.at[i - 1], section=sec(i))
    pieces = jnp.concatenate([KVB[s][:, 0:KW].astype(f32) for s in range(S)], axis=1).astype(bf16)
    window_kv[...] = pieces
    new_low = jnp.where(t_row <= t_col, 0.0, masked_low).astype(f32)
    parts.append(attend(QB[me], pieces[:, 0:HD], pieces[:, HD : 2 * HD], new_low))
    copies[9].wait()
    top = jnp.maximum(parts[0][0], parts[1][0])
    for i in range(1, S):
        arrive(LR.at[i - 1], lss.at[i - 1], lsr.at[i - 1], section=sec(i))
        top = jnp.maximum(top, LR[i - 1, 0:1, :])
    total = jnp.zeros((1, T), f32)
    context = jnp.zeros((HD, T), f32)
    for p in parts:
        weight = jnp.exp(p[0] - top)
        total += weight * p[1]
        context += weight * p[2]
    for i in range(1, S):
        weight = jnp.exp(LR[i - 1, 0:1, :] - top) * LR[i - 1, 8:9, :]
        total += weight
        arrive(ACR.at[i - 1], acs.at[i - 1], acr.at[i - 1], section=sec(i))
        context += weight * ACR[i - 1].astype(f32)
    context = (context / total).T.astype(bf16)

    for c in range(CHUNKS):
        value = jnp.dot(context, Wc[:, c * KC : (c + 1) * KC], preferred_element_type=f32)
        reduce_send(SND2, r2s, r2r, c, value)
        scatter_pairs(SND2, RCV2, r2s, r2r, c)
        if c:
            scatter_sections(SND2, RCV2, r2s, r2r, MID2, RCM2, m2s, m2r, c - 1)
    scatter_sections(SND2, RCV2, r2s, r2r, MID2, RCM2, m2s, m2r, CHUNKS - 1)
    for c in range(CHUNKS):
        cols = slice(c * KC, (c + 1) * KC)
        hidden[:, cols] = (
            RES[:, cols].astype(f32) + scatter_end(MID2, RCM2, m2s, m2r, c)
        ).astype(bf16)
    for d in sent:
        d.wait_send()


def local(
    S, MP,
    tokens, mix_gain, inner_w, gate_w, group_w, step_w, step_bias, rate_log, skip_scale, norm_gain,
    out_w, states, decay, att_gain, query_w, keyval_w, context_w, cache, doc_offset,
):
    rows, D = tokens.shape
    T = rows * S * MP
    KC = D // CHUNKS
    IW = inner_w.shape[1]
    GW = group_w.shape[1]
    heads = step_w.shape[1]
    HP = IW // heads
    NS = states.shape[-1]
    HD = query_w.shape[1]
    dma = pltpu.SemaphoreType.DMA
    vmem = pltpu.VMEM

    def both(*shape):
        return [dma(shape), dma(shape)]

    def scatter():
        return [
            vmem((CHUNKS, MP, S, rows, KC), bf16), vmem((CHUNKS, MP - 1, S, rows, KC), bf16),
            *both(CHUNKS, MP - 1),
            vmem((CHUNKS, S, rows, KC), bf16), vmem((CHUNKS, S - 1, rows, KC), bf16),
            *both(CHUNKS, S - 1),
        ]

    hops = S - 1 + (MP - 1) * S
    scratch = [
        vmem((D, 2 * IW + GW + 128), bf16), vmem(step_w.shape, bf16), vmem(out_w.shape, bf16),
        vmem((D, 2 * HD), bf16), vmem(keyval_w.shape, bf16), vmem(context_w.shape, bf16),
        vmem((cache.shape[0], 2 * HD), bf16), vmem(states.shape[2:], f32), dma((10,)),
        vmem((CHUNKS, S, MP, rows, KC), bf16), vmem((CHUNKS, S, MP, rows, KC), bf16),
        *both(CHUNKS, hops), *both(CHUNKS, hops),
        vmem((T, 2 * IW + GW + 128), f32),
        vmem((S, T, GW), bf16), *both(S - 1),
        vmem((S, IW, NS), bf16), vmem((S, IW, NS), bf16), *both(S - 1),
        vmem((S, 8, 128), f32), *both(S - 1),
        vmem((S, 8, T), f32), *both(S - 1),
        *scatter(), *scatter(),
        vmem((rows, D), bf16),
        vmem((S, T, HD), bf16), *both(S - 1),
        vmem((S, T, HD), bf16), *both(S - 1),
        vmem((S - 1, HD, T), bf16), vmem((S - 1, HD, T), bf16), *both(S - 1),
        vmem((S - 1, 16, T), f32), vmem((S - 1, 16, T), f32), *both(S - 1),
    ]
    v = pl.BlockSpec(memory_space=pltpu.VMEM)
    a = pl.BlockSpec(memory_space=pl.ANY)
    s = pl.BlockSpec(memory_space=pltpu.SMEM)
    hidden, final_state, window_kv = pl.pallas_call(
        functools.partial(kernel, S, MP),
        out_shape=(
            jax.ShapeDtypeStruct((rows, D), bf16),
            jax.ShapeDtypeStruct((heads, HP, NS), f32),
            jax.ShapeDtypeStruct((T, 2 * HD), bf16),
        ),
        in_specs=[v, v, a, a, a, a, s, s, s, v, a, a, v, v, a, a, a, a, s],
        out_specs=(v, v, v),
        scratch_shapes=scratch,
        compiler_params=pltpu.CompilerParams(
            collective_id=0, has_side_effects=True, vmem_limit_bytes=60 * 1024 * 1024
        ),
    )(
        tokens, mix_gain.reshape(1, D), inner_w, gate_w, group_w, step_w, step_bias, rate_log,
        skip_scale, norm_gain.reshape(1, IW), out_w, states, decay, att_gain.reshape(1, D),
        query_w, keyval_w, context_w, cache.reshape(cache.shape[0], 2 * HD), doc_offset,
    )
    return hidden, final_state, window_kv[:, None, :]


def solution(mesh):
    S, MP = mesh.shape["section"], mesh.shape["mp"]
    both = ("section", "mp")
    in_specs = (
        P(("dp", "section", "mp"), None),
        P(),
        P(None, both),
        P(None, both),
        P(None, both),
        P(None, both),
        P(both),
        P(both),
        P(both),
        P(both),
        P(both, None),
        P(("dp", "section"), "mp", None, None, None, None),
        P(("dp", "section"), "mp", None, None),
        P(),
        P(None, both),
        P(None, both),
        P(both, None),
        P(("dp", "section"), "mp", None),
        P("dp"),
    )
    out_specs = (
        P(("dp", "section", "mp"), None),
        P(("dp", "section", "mp"), None, None),
        P("dp", "mp", None),
    )
    return jax.shard_map(
        functools.partial(local, S, MP), mesh=mesh, in_specs=in_specs, out_specs=out_specs, check_vma=False
    )
```

time: 233 us -> 77.3 us (0.33)
  waiting for transfers between devices: 145 us -> 0 us
  Pallas kernels: 0 us -> 62.4 us
  blocking collectives: 25.5 us -> 0 us
  matrix products: 18.7 us -> 0 us
  between operations: 14.7 us -> 1.29 us
  other arithmetic: 12.3 us -> 0 us
  starting transfers between devices: 9.51 us -> 0 us
  local copies, waits for them, and re-layouts: 6.51 us -> 13.1 us
    reduce_scatter x2 -> x0, waiting for transfers between devices: 70 us -> none  [the longest x1 35.5 us: local(): lax.psum_scatter(jnp.dot(normed_heads, out_weight, preferred_element_type...]
    all_gather x3 -> x0, waiting for transfers between devices: 65.2 us -> none  [the longest x1 43.6 us: local(): piece = lax.all_gather(cache_here, 'section', axis=0, tiled=True)]
    pallas_call x0 -> x1, Pallas kernels: none -> 62.4 us  [local(): pl.pallas_call(functools.partial(kernel, S, MP), out_shape=(jax.ShapeDtyp...]
    dot_general x12 -> x0, matrix products: 18.7 us -> none  [the longest x1 5.57 us: local(): jnp.dot(lax.all_gather(normed, ('section', 'mp'), axis=0, tiled=True), fi...]
    all_gather x2 -> x0, blocking collectives: 16.6 us -> none  [the longest x1 8.41 us: local(): paired = lax.all_gather(group_part, 'section', axis=1, tiled=True)]
    all_to_all x2 -> x0, waiting for transfers between devices: 9.65 us -> none  [the longest x1 9.65 us: local(): lax.all_to_all(local_states.astype(jnp.bfloat16), 'section', split_axis=1...]
    all_to_all x2 -> x0, starting transfers between devices: 9.35 us -> none  [the longest x1 5.16 us: local(): lax.all_to_all(local_decay.astype(jnp.bfloat16), 'section', split_axis=1,...]
    psum x1 -> x0, blocking collectives: 8.92 us -> none  [local(): group_squares = lax.psum(row_squares, 'section')]
  transfers between devices with their start and end apart: 7 -> 0, of which waited for: 6 -> 0; matrix products, arithmetic and copies ran while one was open for 6% -> 0% of each run, Pallas kernels for 0% -> 0%
where the time goes in v1:
time: 77.3 us; the launch traced here: 76.8 us
  Pallas kernels  62.4 us (81%)
  local copies, waits for them, and re-layouts  13.1 us (17%)
  between operations  1.29 us (2%)
    pallas_call x1, Pallas kernels, local(): pl.pallas_call(functools.partial(kernel, S, MP), out_shape=(jax.ShapeDtyp...  62.4 us
    unnamed x5, local copies, waits for them, and re-layouts  9.29 us

profile of v1, /device:TPU:0, one launch (start us, length us, event | category | flops | bytes accessed | tf_op | source)
XLA Modules:
  0.0 76.8 jit_solution(5210032295543871598)
XLA Ops:
  1.3 1.2 %reshape.19.norm_gain = bf16[1,256]{1,0:T(2,128)(2,1)} reshape(bf16[256]{0:T(256)(128)(2,1)} %param.28) | data formatting | bytes 1024 | tf_op jit(solution)/shard_map/reshape | solution.py:420
  2.5 1.3 %reshape.18.mix_gain = bf16[1,4096]{1,0:T(2,128)(2,1)} reshape(bf16[4096]{0:T(1024)(128)(2,1)} %param.20) | data formatting | bytes 16384 | tf_op jit(solution)/shard_map/reshape | solution.py:419
  3.8 1.3 %reshape.20.att_gain = bf16[1,4096]{1,0:T(2,128)(2,1)} reshape(bf16[4096]{0:T(1024)(128)(2,1)} %param.32) | data formatting | bytes 16384 | tf_op jit(solution)/shard_map/reshape | solution.py:420
  5.1 2.2 %copy.22.step_w = bf16[4096,4]{1,0:T(8,128)(2,1)} copy(bf16[4096,4]{0,1:T(4,128)(2,1)} %param.24) | data formatting | bytes 65536 | tf_op args[5]
  7.3 2.4 %copy.23.keyval_w = bf16[4096,64]{1,0:T(8,128)(2,1)} copy(bf16[4096,64]{0,1:T(8,128)(2,1)} %param.34) | data formatting | bytes 1048576 | tf_op args[15]
  9.7 62.4 %shard_map.202 = (bf16[16,4096]{1,0:T(8,128)(2,1)}, f32[4,64,256]{2,1,0:T(8,128)}, bf16[128,256]{1,0:T(8,128)(2,1)}) custom-call(bf16[16,4096]{1,0:T(8,128)(2,1)} %tokens.1, bf16[1,4096]{1,0:T(2,128)(2,1)} %reshape.18.mix_gain, bf16[4096,256]{1,0:T(8,128)(2,1)} %inner_w.1, bf16[4096,256]{1,0:T(8,128)(2,1)} %gate_w.1, bf16[4096,128]{1,0:T(8,128)(2,1)} %group_w.1, ...), custom_call_target="tpu_custom_call" | custom-call | tf_op jit(solution)/shard_map/pallas_call | solution.py:405
  72.1 1.6 %copy.28 = bf16[16,4096]{1,0:T(8,128)(2,1)} copy(bf16[16,4096]{1,0:T(8,128)(2,1)} %get-tuple-element.12) | data formatting | bytes 262144
  73.7 1.7 %copy.29 = f32[4,64,256]{2,1,0:T(8,128)} copy(f32[4,64,256]{2,1,0:T(8,128)} %get-tuple-element.13) | data formatting | bytes 524288
  75.3 1.5 %copy.30 = bf16[128,1,256]{2,0,1:T(8,128)(2,1)} copy(bf16[128,1,256]{2,0,1:T(8,128)(2,1)} %bitcast.3) | data formatting | bytes 131072

commit v2 on v1

--- a/solution.py
+++ b/solution.py
@@ -25,7 +25,7 @@
     tokens, mix_gain, inner_w, gate_w, group_w, step_w, step_bias, rate_log, skip_scale, norm_gain,
     out_w, states, decay, att_gain, query_w, keyval_w, context_w, cache, doc_offset,
     hidden, final_state, window_kv,
-    W1, WS, Wo, W2, WKV, Wc, CK, SF, load_sem,
+    W1, Wo, W2, WKV, Wc, CK, SF, load_sem,
     G1, G2, g1s, g1r, g2s, g2r,
     acc, GP, gps, gpr, STS, ST, sts, str_, DB, dbs, dbr, SQ, sqs, sqr,
     SND1, RCV1, r1s, r1r, MID1, RCM1, m1s, m1r,
@@ -39,10 +39,10 @@
     KC = D // CHUNKS
     IW = inner_w.shape[1]
     GW = group_w.shape[1]
-    heads = step_w.shape[1]
+    heads = step_w.shape[0]
     HP = IW // heads
     HD = query_w.shape[1]
-    KW = keyval_w.shape[1]
+    KW = keyval_w.shape[0]
     sent = []
 
     def sec(i):
@@ -68,10 +68,9 @@
         (inner_w, W1.at[:, 0:IW]),
         (gate_w, W1.at[:, IW : 2 * IW]),
         (group_w, W1.at[:, 2 * IW : 2 * IW + GW]),
-        (step_w, WS),
         (states.at[0, 0], SF),
         (out_w, Wo),
-        (query_w, W2.at[:, 0:HD]),
+        (query_w, W2),
         (keyval_w, WKV),
         (cache, CK),
         (context_w, Wc),
@@ -101,26 +100,28 @@
                 k = S - 1 + (j - 1) * S
                 send(own, own, ss.at[c, k], rs.at[c, k], mp=core(j))
 
-    def gather_chunk(G, ss, rs, c):
+    def gather_pass(G, ss, rs, c):
         for i in range(1, S):
             got = G.at[c, sec(-i), mm]
             arrive(got, ss.at[c, i - 1], rs.at[c, i - 1], section=sec(i))
             for j in range(1, MP):
                 k = S - 1 + (j - 1) * S + i
                 send(got, got, ss.at[c, k], rs.at[c, k], mp=core(j))
+
+    def gather_end(G, ss, rs, c):
         for j in range(1, MP):
             for i in range(S):
                 k = S - 1 + (j - 1) * S + i
                 got = G.at[c, sec(-i), core(-j)]
                 arrive(got, ss.at[c, k], rs.at[c, k], mp=core(j))
 
-    norm_into(G1, tokens[...].astype(f32), mix_gain[...].astype(f32))
+    norm_into(G1, tokens[...].astype(f32), mix_gain[...].astype(f32).reshape(1, D))
     DB[me] = jnp.zeros(DB.shape[1:], f32)
     DB[me, 0:S, 0:heads] = decay[0, 0]
     pl.semaphore_wait(barrier, S - 1 + MP - 1)
     gather_start(G1, g1s, g1r)
 
-    copies[4].wait()
+    copies[3].wait()
     for q in range(S):
         STS[q] = SF[q].reshape(IW, SF.shape[-1]).astype(bf16)
     ST[me] = STS[me]
@@ -128,28 +129,28 @@
         send(DB.at[me], DB.at[me], dbs.at[i - 1], dbr.at[i - 1], section=sec(i))
         send(STS.at[sec(i)], ST.at[me], sts.at[i - 1], str_.at[i - 1], section=sec(i))
 
-    copies[3].wait()
-    W1[:, 2 * IW + GW :] = jnp.zeros((D, W1.shape[1] - 2 * IW - GW), bf16)
-    W1[:, 2 * IW + GW : 2 * IW + GW + heads] = WS[...]
-    copies[7].wait()
-    W2[:, HD:] = jnp.zeros((D, W2.shape[1] - HD), bf16)
-    W2[:, HD : HD + KW] = WKV[...]
     for k in (0, 1, 2):
         copies[k].wait()
 
-    def project(G, ss, rs, W):
-        total = None
+    def project(G, ss, rs, W, side):
+        wide, extra = W.shape[1], side.shape[0]
+        gather_pass(G, ss, rs, 0)
         for c in range(CHUNKS):
-            gather_chunk(G, ss, rs, c)
-            part = jnp.dot(
-                G[c].reshape(T, KC), W[c * KC : (c + 1) * KC, :], preferred_element_type=f32
-            )
+            if c + 1 < CHUNKS:
+                gather_pass(G, ss, rs, c + 1)
+            gather_end(G, ss, rs, c)
+            rowsets = G[c].reshape(T, KC)
+            part = jnp.dot(rowsets, W[c * KC : (c + 1) * KC, :], preferred_element_type=f32)
+            more = dot(rowsets, side[:, c * KC : (c + 1) * KC], 1, 1)
             if c == 0:
-                acc[:, 0 : W.shape[1]] = part
+                acc[:, 0:wide] = part
+                acc[:, wide : wide + extra] = more
             else:
-                acc[:, 0 : W.shape[1]] += part
-
-    project(G1, g1s, g1r, W1)
+                acc[:, 0:wide] += part
+                acc[:, wide : wide + extra] += more
+
+    acc[:, 2 * IW + GW :] = jnp.zeros((T, 128), f32)
+    project(G1, g1s, g1r, W1, step_w)
     GP[me] = acc[:, 2 * IW : 2 * IW + GW].astype(bf16)
     for i in range(1, S):
         send(GP.at[me], GP.at[me], gps.at[i - 1], gpr.at[i - 1], section=sec(i))
@@ -217,7 +218,7 @@
     SQ[me] = dot(jnp.ones((8, IW), f32), gated * gated, 1, 1, precision=lax.Precision.HIGHEST)
     for i in range(1, S):
         send(SQ.at[me], SQ.at[me], sqs.at[i - 1], sqr.at[i - 1], section=sec(i))
-    lhs = (gated * norm_gain[...].astype(f32)).astype(bf16)
+    lhs = (gated * norm_gain[...].astype(f32).reshape(1, IW)).astype(bf16)
 
     def reduce_send(SND, ss, rs, c, value):
         value = value.astype(bf16).reshape(S, MP, rows, KC)
@@ -246,7 +247,7 @@
             total += RCM[c, i - 1].astype(f32)
         return total
 
-    copies[5].wait()
+    copies[4].wait()
     inverse = None
     for c in range(CHUNKS):
         value = jnp.dot(lhs, Wo[:, c * KC : (c + 1) * KC], preferred_element_type=f32)
@@ -274,11 +275,12 @@
         RES[:, cols] = (
             tokens[:, cols].astype(f32) + scatter_end(MID1, RCM1, m1s, m1r, c)
         ).astype(bf16)
-    norm_into(G2, RES[...].astype(f32), att_gain[...].astype(f32))
+    norm_into(G2, RES[...].astype(f32), att_gain[...].astype(f32).reshape(1, D))
     gather_start(G2, g2s, g2r)
-    copies[6].wait()
-    copies[8].wait()
-    project(G2, g2s, g2r, W2)
+    for k in (5, 6, 7):
+        copies[k].wait()
+    acc[:, HD : 2 * HD] = jnp.zeros((T, HD), f32)
+    project(G2, g2s, g2r, W2, WKV)
     QB[me] = acc[:, 0:HD].astype(bf16)
     for i in range(1, S):
         send(QB.at[me], QB.at[me], qbs.at[i - 1], qbr.at[i - 1], section=sec(i))
@@ -318,7 +320,7 @@
     window_kv[...] = pieces
     new_low = jnp.where(t_row <= t_col, 0.0, masked_low).astype(f32)
     parts.append(attend(QB[me], pieces[:, 0:HD], pieces[:, HD : 2 * HD], new_low))
-    copies[9].wait()
+    copies[8].wait()
     top = jnp.maximum(parts[0][0], parts[1][0])
     for i in range(1, S):
         arrive(LR.at[i - 1], lss.at[i - 1], lsr.at[i - 1], section=sec(i))
@@ -350,6 +352,14 @@
         ).astype(bf16)
     for d in sent:
         d.wait_send()
+
+
+def copy_kernel(a, b, c, x, y, z, sem):
+    copies = [pltpu.make_async_copy(p, q, sem.at[k]) for k, (p, q) in enumerate(((a, x), (b, y), (c, z)))]
+    for d in copies:
+        d.start()
+    for d in copies:
+        d.wait()
 
 
 def local(
@@ -382,9 +392,9 @@
 
     hops = S - 1 + (MP - 1) * S
     scratch = [
-        vmem((D, 2 * IW + GW + 128), bf16), vmem(step_w.shape, bf16), vmem(out_w.shape, bf16),
-        vmem((D, 2 * HD), bf16), vmem(keyval_w.shape, bf16), vmem(context_w.shape, bf16),
-        vmem((cache.shape[0], 2 * HD), bf16), vmem(states.shape[2:], f32), dma((10,)),
+        vmem((D, 2 * IW + GW), bf16), vmem(out_w.shape, bf16),
+        vmem((D, HD), bf16), vmem(keyval_w.shape[::-1], bf16), vmem(context_w.shape, bf16),
+        vmem((cache.shape[0], 2 * HD), bf16), vmem(states.shape[2:], f32), dma((9,)),
         vmem((CHUNKS, S, MP, rows, KC), bf16), vmem((CHUNKS, S, MP, rows, KC), bf16),
         *both(CHUNKS, hops), *both(CHUNKS, hops),
         vmem((T, 2 * IW + GW + 128), f32),
@@ -409,17 +419,25 @@
             jax.ShapeDtypeStruct((heads, HP, NS), f32),
             jax.ShapeDtypeStruct((T, 2 * HD), bf16),
         ),
-        in_specs=[v, v, a, a, a, a, s, s, s, v, a, a, v, v, a, a, a, a, s],
+        in_specs=[v, v, a, a, a, v, s, s, s, v, a, a, v, v, a, a, a, a, s],
         out_specs=(v, v, v),
         scratch_shapes=scratch,
         compiler_params=pltpu.CompilerParams(
             collective_id=0, has_side_effects=True, vmem_limit_bytes=60 * 1024 * 1024
         ),
     )(
-        tokens, mix_gain.reshape(1, D), inner_w, gate_w, group_w, step_w, step_bias, rate_log,
-        skip_scale, norm_gain.reshape(1, IW), out_w, states, decay, att_gain.reshape(1, D),
-        query_w, keyval_w, context_w, cache.reshape(cache.shape[0], 2 * HD), doc_offset,
+        tokens, mix_gain, inner_w, gate_w, group_w, step_w.T, step_bias, rate_log,
+        skip_scale, norm_gain, out_w, states, decay, att_gain,
+        query_w, keyval_w.T, context_w, cache.reshape(cache.shape[0], 2 * HD), doc_offset,
     )
+    results = (hidden, final_state, window_kv)
+    hidden, final_state, window_kv = pl.pallas_call(
+        copy_kernel,
+        out_shape=tuple(jax.ShapeDtypeStruct(x.shape, x.dtype) for x in results),
+        in_specs=[a, a, a],
+        out_specs=(a, a, a),
+        scratch_shapes=[dma((3,))],
+    )(*results)
     return hidden, final_state, window_kv[:, None, :]
 
 

time: 77.3 us -> 79.1 us (1.023)
  Pallas kernels: 62.4 us -> 77.7 us
  local copies, waits for them, and re-layouts: 13.1 us -> 0 us
    pallas_call x0 -> x1, Pallas kernels: none -> 15 us  [local(): pl.pallas_call(copy_kernel, out_shape=tuple((jax.ShapeDtypeStruct(x.shape...]
    unnamed x5 -> x0, local copies, waits for them, and re-layouts: 9.29 us -> none
    reshape x3 -> x0, local copies, waits for them, and re-layouts: 3.84 us -> none  [the longest x1 1.31 us: local(): mix_gain.reshape(1, D)]
where the time goes in v2:
time: 79.1 us; the launch traced here: 79 us
  Pallas kernels  77.7 us (98%)
  between operations  1.29 us (2%)
    pallas_call x1, Pallas kernels, local(): pl.pallas_call(functools.partial(kernel, S, MP), out_shape=(jax.ShapeDtyp...  62.6 us
    pallas_call x1, Pallas kernels, local(): pl.pallas_call(copy_kernel, out_shape=tuple((jax.ShapeDtypeStruct(x.shape...  15 us

profile of v2, /device:TPU:0, one launch (start us, length us, event | category | flops | bytes accessed | tf_op | source)
XLA Modules:
  0.0 79.0 jit_solution(13660798462683401869)
XLA Ops:
  1.3 62.6 %shard_map.202 = (bf16[16,4096]{1,0:T(8,128)(2,1)}, f32[4,64,256]{2,1,0:T(8,128)}, bf16[128,256]{1,0:T(8,128)(2,1)}) custom-call(bf16[16,4096]{1,0:T(8,128)(2,1)} %tokens.1, bf16[4096]{0:T(1024)(128)(2,1)} %mix_gain.1, bf16[4096,256]{1,0:T(8,128)(2,1)} %inner_w.1, bf16[4096,256]{1,0:T(8,128)(2,1)} %gate_w.1, bf16[4096,128]{1,0:T(8,128)(2,1)} %group_w.1, ...), custom_call_target="tpu_custom_call" | custom-call | tf_op jit(solution)/shard_map/pallas_call | solution.py:415
  63.9 15.0 %shard_map.203 = (bf16[16,4096]{1,0:T(8,128)(2,1)}, f32[4,64,256]{2,1,0:T(8,128)}, bf16[128,256]{1,0:T(8,128)(2,1)}) custom-call(bf16[16,4096]{1,0:T(8,128)(2,1)} %get-tuple-element.9.a, f32[4,64,256]{2,1,0:T(8,128)} %get-tuple-element.10.b, bf16[128,256]{1,0:T(8,128)(2,1)} %get-tuple-element.11.c), custom_call_target="tpu_custom_call" | custom-call | tf_op jit(solution)/shard_map/pallas_call | solution.py:434

commit v3 on v2

--- a/solution.py
+++ b/solution.py
@@ -354,12 +354,17 @@
         d.wait_send()
 
 
-def copy_kernel(a, b, c, x, y, z, sem):
-    copies = [pltpu.make_async_copy(p, q, sem.at[k]) for k, (p, q) in enumerate(((a, x), (b, y), (c, z)))]
-    for d in copies:
+def copy_kernel(a, b, c, x, y, z, i, j, k, sem):
+    trips = ((a, i, x), (b, j, y), (c, k, z))
+    loads = [pltpu.make_async_copy(src, mid, sem.at[n]) for n, (src, mid, _) in enumerate(trips)]
+    stores = [pltpu.make_async_copy(mid, dst, sem.at[n + 3]) for n, (_, mid, dst) in enumerate(trips)]
+    for d in loads:
         d.start()
-    for d in copies:
+    for d, e in zip(loads, stores):
         d.wait()
+        e.start()
+    for e in stores:
+        e.wait()
 
 
 def local(
@@ -436,7 +441,7 @@
         out_shape=tuple(jax.ShapeDtypeStruct(x.shape, x.dtype) for x in results),
         in_specs=[a, a, a],
         out_specs=(a, a, a),
-        scratch_shapes=[dma((3,))],
+        scratch_shapes=[*(vmem(x.shape, x.dtype) for x in results), dma((6,))],
     )(*results)
     return hidden, final_state, window_kv[:, None, :]
 

time: 79.1 us -> 65.9 us (0.83)
  Pallas kernels: 77.7 us -> 64.4 us
    pallas_call x1, Pallas kernels: 15 us -> 1.79 us  [local(): pl.pallas_call(copy_kernel, out_shape=tuple((jax.ShapeDtypeStruct(x.shape...]
where the time goes in v3:
time: 65.9 us; the launch traced here: 65.7 us
  Pallas kernels  64.4 us (98%)
  between operations  1.29 us (2%)
    pallas_call x1, Pallas kernels, local(): pl.pallas_call(functools.partial(kernel, S, MP), out_shape=(jax.ShapeDtyp...  62.6 us
    pallas_call x1, Pallas kernels, local(): pl.pallas_call(copy_kernel, out_shape=tuple((jax.ShapeDtypeStruct(x.shape...  1.79 us

profile of v3, /device:TPU:0, one launch (start us, length us, event | category | flops | bytes accessed | tf_op | source)
XLA Modules:
  0.0 65.7 jit_solution(8185241728992424598)
XLA Ops:
  1.3 62.6 %shard_map.202 = (bf16[16,4096]{1,0:T(8,128)(2,1)}, f32[4,64,256]{2,1,0:T(8,128)}, bf16[128,256]{1,0:T(8,128)(2,1)}) custom-call(bf16[16,4096]{1,0:T(8,128)(2,1)} %tokens.1, bf16[4096]{0:T(1024)(128)(2,1)} %mix_gain.1, bf16[4096,256]{1,0:T(8,128)(2,1)} %inner_w.1, bf16[4096,256]{1,0:T(8,128)(2,1)} %gate_w.1, bf16[4096,128]{1,0:T(8,128)(2,1)} %group_w.1, ...), custom_call_target="tpu_custom_call" | custom-call | tf_op jit(solution)/shard_map/pallas_call | solution.py:420
  63.9 1.8 %shard_map.203 = (bf16[16,4096]{1,0:T(8,128)(2,1)}, f32[4,64,256]{2,1,0:T(8,128)}, bf16[128,256]{1,0:T(8,128)(2,1)}) custom-call(bf16[16,4096]{1,0:T(8,128)(2,1)} %get-tuple-element.9.a, f32[4,64,256]{2,1,0:T(8,128)} %get-tuple-element.10.b, bf16[128,256]{1,0:T(8,128)(2,1)} %get-tuple-element.11.c), custom_call_target="tpu_custom_call" | custom-call | tf_op jit(solution)/shard_map/pallas_call | solution.py:439

commit v4 on v3

--- a/solution.py
+++ b/solution.py
@@ -13,7 +13,7 @@
 MESH = pl.DeviceIdType.MESH
 f32 = jnp.float32
 bf16 = jnp.bfloat16
-CHUNKS = 4
+CHUNKS = 2
 
 
 def dot(a, b, ca, cb, **kw):

time: 65.9 us -> 65.5 us (level)
  no operation moved by 1% of the time
where the time goes in v4:
time: 65.5 us; the launch traced here: 65.3 us
  Pallas kernels  64 us (98%)
  between operations  1.29 us (2%)
    pallas_call x1, Pallas kernels, local(): pl.pallas_call(functools.partial(kernel, S, MP), out_shape=(jax.ShapeDtyp...  62.2 us
    pallas_call x1, Pallas kernels, local(): pl.pallas_call(copy_kernel, out_shape=tuple((jax.ShapeDtypeStruct(x.shape...  1.79 us

profile of v4, /device:TPU:0, one launch (start us, length us, event | category | flops | bytes accessed | tf_op | source)
XLA Modules:
  0.0 65.3 jit_solution(5137547755002550224)
XLA Ops:
  1.3 62.2 %shard_map.202 = (bf16[16,4096]{1,0:T(8,128)(2,1)}, f32[4,64,256]{2,1,0:T(8,128)}, bf16[128,256]{1,0:T(8,128)(2,1)}) custom-call(bf16[16,4096]{1,0:T(8,128)(2,1)} %tokens.1, bf16[4096]{0:T(1024)(128)(2,1)} %mix_gain.1, bf16[4096,256]{1,0:T(8,128)(2,1)} %inner_w.1, bf16[4096,256]{1,0:T(8,128)(2,1)} %gate_w.1, bf16[4096,128]{1,0:T(8,128)(2,1)} %group_w.1, ...), custom_call_target="tpu_custom_call" | custom-call | tf_op jit(solution)/shard_map/pallas_call | solution.py:420
  63.5 1.8 %shard_map.203 = (bf16[16,4096]{1,0:T(8,128)(2,1)}, f32[4,64,256]{2,1,0:T(8,128)}, bf16[128,256]{1,0:T(8,128)(2,1)}) custom-call(bf16[16,4096]{1,0:T(8,128)(2,1)} %get-tuple-element.9.a, f32[4,64,256]{2,1,0:T(8,128)} %get-tuple-element.10.b, bf16[128,256]{1,0:T(8,128)(2,1)} %get-tuple-element.11.c), custom_call_target="tpu_custom_call" | custom-call | tf_op jit(solution)/shard_map/pallas_call | solution.py:439
